TPU v7x, 512 devices: a whole 4x4x16 slice. The times are simulated.
512 devices in a mesh: domain: 8 (over x, core), fsdp: 64 (over y, z).
Axes of the slice: x: 4, y: 4, z: 16, core: 2. Of those that a mesh axis runs over, the one named last changes fastest.
Arguments:
- gradients: bfloat16 [8, 64, 4096, 512], P('domain', None, 'fsdp')
- row_counts: int32 [64], replicated, may hold values from 2048 to 4096, as said below
- domain_ids: int32 [8], replicated, may hold values from 0 to 7
- domain_weights: float32 [8], replicated, may hold values from 0.2 to 2
Outputs:
- updates: float32 [64, 4096, 512], P('domain', 'fsdp')
- new_weights: float32 [8], replicated
Inputs may be any that keep to these rules, and one draw needn't show every extreme that they name: `row_counts`: each matrix has 4096 or 2048 rows, and both counts occur.
All inputs are finite; a program needn't handle non-finite values.
Results may differ from a plain program's by a relative error of at most 0.0071.
Values may be sent and summed in bfloat16 or wider, within the bound.
A program may use at most 64 MiB of HBM per device.

v0:
```python
import math
import jax
import jax.numpy as jnp
from jax import lax
from jax.sharding import PartitionSpec as P

NS_ITERS = 3
OWNERS = 8
COEF_A = 3.4445
COEF_B = -4.775
COEF_C = 2.0315
MUON_SCALE = 0.2
ETA = 4.0


def partner(shard, axis, stride):
    return lax.ppermute(shard, axis, [(i, i ^ 1 << stride) for i in range(lax.axis_size(axis))])


def group_mixing(domain_ids, domain_weights, kind_count):
    weight_share = domain_weights / jnp.sum(domain_weights)
    onehot = (domain_ids[:, None] == jnp.arange(kind_count, dtype=jnp.int32)[None, :]).astype(
        jnp.float32
    )
    counts = jnp.sum(onehot, axis=0)
    per_member = weight_share / jnp.maximum(counts, 1.0)
    group_mix = jnp.sum(onehot * per_member[None, :], axis=1)
    return (weight_share, onehot, counts, group_mix)


def summed_gram(iterate):
    gram_total = lax.dot_general(
        iterate, iterate, (((0,), (0,)), ((), ())), preferred_element_type=jnp.float32
    )
    for bit_pos in range(OWNERS.bit_length() - 1):
        gram_total = gram_total + partner(gram_total, "fsdp", bit_pos)
    return gram_total


def newton_steps(iterate):
    for repeat in range(NS_ITERS):
        gram_full = lax.optimization_barrier(summed_gram(iterate).astype(jnp.bfloat16))
        square = jnp.dot(gram_full, gram_full, preferred_element_type=jnp.float32)
        poly_term = (COEF_B * gram_full.astype(jnp.float32) + COEF_C * square).astype(jnp.bfloat16)
        iterate = lax.optimization_barrier(
            (
                COEF_A * iterate.astype(jnp.float32)
                + jnp.dot(iterate, poly_term, preferred_element_type=jnp.float32)
            ).astype(jnp.bfloat16)
        )
    return iterate


def share_scores(aligned, squares, norm_slots):
    return lax.psum((aligned, squares, norm_slots), ("domain", "fsdp"))


def body(gradients, row_counts, domain_ids, domain_weights):
    groups = lax.axis_size("domain")
    shards = lax.axis_size("fsdp")
    matrices = row_counts.shape[0]
    rows_src = gradients.shape[2]
    columns = gradients.shape[3]
    per_domain = matrices // groups
    sub_rows = rows_src // OWNERS
    own_rows = shards * sub_rows
    full_rows = rows_src * shards
    domain_pos = lax.axis_index("domain")
    shard_pos = lax.axis_index("fsdp")
    matrix_index = domain_pos * per_domain + shard_pos // OWNERS
    owner_rank = shard_pos % OWNERS
    source = jnp.arange(shards, dtype=jnp.int32)[:, None]
    within = jnp.arange(sub_rows, dtype=jnp.int32)[None, :]
    owner_rows = (source * rows_src + owner_rank * sub_rows + within).reshape(own_rows)
    weight_share, onehot, counts, group_mix = group_mixing(
        domain_ids, domain_weights, domain_weights.shape[0]
    )
    sectioned = gradients.reshape(1, groups, shards, sub_rows, columns)
    received = lax.all_to_all(
        lax.all_to_all(sectioned, "domain", split_axis=1, concat_axis=0, tiled=True),
        "fsdp",
        split_axis=2,
        concat_axis=3,
        tiled=True,
    )
    received = received.reshape(groups, own_rows, columns)
    row_limit = lax.dynamic_index_in_dim(row_counts, matrix_index, 0, keepdims=False)
    row_mask = (owner_rows < row_limit)[None, :, None]
    masked = jnp.where(row_mask, received.astype(jnp.float32), jnp.zeros((), jnp.float32))
    combined = jnp.sum(group_mix[:, None, None] * masked, axis=0)
    aligned = jnp.sum(masked * combined[None], axis=(1, 2))
    squares = jnp.sum(masked * masked, axis=(1, 2))
    own_square = jnp.sum(combined * combined)
    norm_slots = jnp.where(
        jnp.arange(matrices, dtype=jnp.int32) == matrix_index,
        own_square,
        jnp.zeros((), jnp.float32),
    )
    aligned, squares, norm_slots = share_scores(aligned, squares, norm_slots)
    frob_norm = (
        jnp.sqrt(lax.dynamic_index_in_dim(norm_slots, matrix_index, 0, keepdims=False)) + 1e-07
    )
    start_rows = lax.optimization_barrier((combined / frob_norm).astype(jnp.bfloat16))
    finished = newton_steps(start_rows)
    returned = lax.all_to_all(
        finished.reshape(1, shards, sub_rows, columns),
        "fsdp",
        split_axis=1,
        concat_axis=0,
        tiled=True,
    )
    returned = returned.reshape(per_domain, rows_src, columns)
    updates = returned.astype(jnp.float32) * (MUON_SCALE * math.sqrt(full_rows))
    total_sq = jnp.sum(norm_slots)
    cosine = aligned / (jnp.sqrt(squares) * jnp.sqrt(total_sq) + 1e-06)
    score = jnp.sum(onehot * cosine[:, None], axis=0) / jnp.maximum(counts, 1.0)
    raised = weight_share * jnp.exp(ETA * score)
    return (updates, raised / jnp.sum(raised))


def solution(mesh):
    placed = (P("domain", None, "fsdp", None), P(), P(), P())
    return jax.shard_map(
        body,
        mesh=mesh,
        in_specs=placed,
        out_specs=(P("domain", "fsdp", None), P()),
        check_vma=False,
    )
```

profile of v0, /device:TPU:8, one launch (start us, length us, event | category | flops | bytes accessed | tf_op | source)
XLA Modules:
  0.0 937.1 jit_solution(9981151052940490858)
XLA Ops:
  0.6 54.6 %all_to_all.30 = bf16[1,8,64,8,512]{4,3,2,0,1:T(8,128)(2,1)S(1)} all-to-all(bf16[1,8,64,8,512]{4,3,2,0,1:T(8,128)(2,1)} %bitcast.26), channel_id=1, replica_groups=mesh['domain'=8,'fsdp'=64] {'domain'}, dimensions={1} | all-to-all | bytes 8388608 | tf_op jit(solution)/shard_map/all_to_all | solution.py:80
  55.3 2.6 copy.8
  57.9 19.1 %all-to-all-start.1 = ((bf16[8,1,64,8,512]{4,3,0,1,2:T(8,128)(2,1)}), bf16[8,1,64,8,512]{4,3,0,1,2:T(8,128)(2,1)}, u32[]{:S(2)}, u32[]{:S(2)}) async-start(bf16[8,1,64,8,512]{4,3,0,1,2:T(8,128)(2,1)} %copy.8), calls=%async_computation.1 | async-start | bytes 8388608 | tf_op jit(solution)/shard_map/all_to_all | solution.py:79
  79.8 182.4 %all-to-all-done.1 = bf16[8,1,64,8,512]{4,3,0,1,2:T(8,128)(2,1)} async-done(((bf16[8,1,64,8,512]{4,3,0,1,2:T(8,128)(2,1)}), bf16[8,1,64,8,512]{4,3,0,1,2:T(8,128)(2,1)}, u32[]{:S(2)}, u32[]{:S(2)}) %all-to-all-start.1) | async-done | bytes 4194336 | tf_op jit(solution)/shard_map/all_to_all | solution.py:79
  262.2 4.3 multiply_reduce_fusion.2
  268.0 4.3 multiply_reduce_fusion
  272.3 99.8 %all-reduce = (f32[64]{0:T(128)S(1)}, f32[8]{0:T(128)S(1)}, f32[8]{0:T(128)S(1)}) all-reduce(f32[64]{0:T(128)S(1)} %compare_select_fusion, f32[8]{0:T(128)S(1)} %get-tuple-element.3, f32[8]{0:T(128)S(1)} %get-tuple-element.2), channel_id=1, replica_groups=mesh['domain'=8,'fsdp'=64] {'domain','fsdp'}, use_global_device_ids=true, to_apply=%region_5.6 | all-reduce | flops 80 | bytes 640 | tf_op jit(solution)/shard_map/psum | solution.py:55
  374.0 3.8 collective-permute-start
  377.7 23.2 %collective-permute-done = f32[512,512]{1,0:T(8,128)S(1)} collective-permute-done((f32[512,512]{1,0:T(8,128)S(1)}, f32[512,512]{1,0:T(8,128)S(1)}, u32[]{:S(2)}, u32[]{:S(2)}) %collective-permute-start) | collective-permute-done | bytes 1048608 | tf_op jit(solution)/shard_map/ppermute | solution.py:17
  401.1 3.1 collective-permute-start.1
  404.1 46.4 %collective-permute-done.1 = f32[512,512]{1,0:T(8,128)S(1)} collective-permute-done((f32[512,512]{1,0:T(8,128)S(1)}, f32[512,512]{1,0:T(8,128)S(1)}, u32[]{:S(2)}, u32[]{:S(2)}) %collective-permute-start.1) | collective-permute-done | bytes 1048608 | tf_op jit(solution)/shard_map/ppermute | solution.py:17
  450.7 5.4 collective-permute-start.2
  456.1 90.8 %collective-permute-done.2 = f32[512,512]{1,0:T(8,128)S(1)} collective-permute-done((f32[512,512]{1,0:T(8,128)S(1)}, f32[512,512]{1,0:T(8,128)S(1)}, u32[]{:S(2)}, u32[]{:S(2)}) %collective-permute-start.2) | collective-permute-done | bytes 1048608 | tf_op jit(solution)/shard_map/ppermute | solution.py:17
  548.4 1.9 collective-permute-start.3
  550.3 25.0 %collective-permute-done.3 = f32[512,512]{1,0:T(8,128)S(1)} collective-permute-done((f32[512,512]{1,0:T(8,128)S(1)}, f32[512,512]{1,0:T(8,128)S(1)}, u32[]{:S(2)}, u32[]{:S(2)}) %collective-permute-start.3) | collective-permute-done | bytes 1048608 | tf_op jit(solution)/shard_map/ppermute | solution.py:17
  577.5 47.6 %collective-permute-done.4 = f32[512,512]{1,0:T(8,128)S(1)} collective-permute-done((f32[512,512]{1,0:T(8,128)S(1)}, f32[512,512]{1,0:T(8,128)S(1)}, u32[]{:S(2)}, u32[]{:S(2)}) %collective-permute-start.4) | collective-permute-done | bytes 1048608 | tf_op jit(solution)/shard_map/ppermute | solution.py:17
  625.3 3.6 collective-permute-start.5
  628.9 90.8 %collective-permute-done.5 = f32[512,512]{1,0:T(8,128)S(1)} collective-permute-done((f32[512,512]{1,0:T(8,128)S(1)}, f32[512,512]{1,0:T(8,128)S(1)}, u32[]{:S(2)}, u32[]{:S(2)}) %collective-permute-start.5) | collective-permute-done | bytes 1048608 | tf_op jit(solution)/shard_map/ppermute | solution.py:17
  723.2 25.0 %collective-permute-done.6 = f32[512,512]{1,0:T(8,128)S(1)} collective-permute-done((f32[512,512]{1,0:T(8,128)S(1)}, f32[512,512]{1,0:T(8,128)S(1)}, u32[]{:S(2)}, u32[]{:S(2)}) %collective-permute-start.6) | collective-permute-done | bytes 1048608 | tf_op jit(solution)/shard_map/ppermute | solution.py:17
  750.4 47.6 %collective-permute-done.7 = f32[512,512]{1,0:T(8,128)S(1)} collective-permute-done((f32[512,512]{1,0:T(8,128)S(1)}, f32[512,512]{1,0:T(8,128)S(1)}, u32[]{:S(2)}, u32[]{:S(2)}) %collective-permute-start.7) | collective-permute-done | bytes 1048608 | tf_op jit(solution)/shard_map/ppermute | solution.py:17
  798.1 3.6 collective-permute-start.8
  801.7 90.8 %collective-permute-done.8 = f32[512,512]{1,0:T(8,128)S(1)} collective-permute-done((f32[512,512]{1,0:T(8,128)S(1)}, f32[512,512]{1,0:T(8,128)S(1)}, u32[]{:S(2)}, u32[]{:S(2)}) %collective-permute-start.8) | collective-permute-done | bytes 1048608 | tf_op jit(solution)/shard_map/ppermute | solution.py:17
  894.3 9.8 %all-to-all-start.2 = ((bf16[1,64,8,512]{3,2,0,1:T(8,128)(2,1)}), bf16[1,64,8,512]{3,2,0,1:T(8,128)(2,1)S(1)}, u32[]{:S(2)}, u32[]{:S(2)}) async-start(bf16[1,64,8,512]{3,2,0,1:T(8,128)(2,1)} %bitcast.6), calls=%async_computation.2 | async-start | bytes 1048576 | tf_op jit(solution)/shard_map/all_to_all | solution.py:105
  908.2 27.8 %all-to-all-done.2 = bf16[1,64,8,512]{3,2,0,1:T(8,128)(2,1)S(1)} async-done(((bf16[1,64,8,512]{3,2,0,1:T(8,128)(2,1)}), bf16[1,64,8,512]{3,2,0,1:T(8,128)(2,1)S(1)}, u32[]{:S(2)}, u32[]{:S(2)}) %all-to-all-start.2) | async-done | bytes 524320 | tf_op jit(solution)/shard_map/all_to_all | solution.py:105
  (41 shorter events, 21.8 us)
Async XLA Ops:
  57.9 19.1 %copy-start = (f32[8]{0:T(128)S(1)}, f32[8]{0:T(128)}, u32[]{:S(2)}) copy-start(f32[8]{0:T(128)} %param.7) | copy-start | bytes 100
  57.9 19.7 %copy-start.1 = (s32[64]{0:T(128)S(1)}, s32[64]{0:T(128)}, u32[]{:S(2)}) copy-start(s32[64]{0:T(128)} %param.5) | copy-start | bytes 772
  57.9 20.3 %copy-start.2 = (s32[8]{0:T(128)S(1)}, s32[8]{0:T(128)}, u32[]{:S(2)}) copy-start(s32[8]{0:T(128)} %param.6) | copy-start | bytes 100
  57.9 204.3 %all-to-all-start.1 = ((bf16[8,1,64,8,512]{4,3,0,1,2:T(8,128)(2,1)}), bf16[8,1,64,8,512]{4,3,0,1,2:T(8,128)(2,1)}, u32[]{:S(2)}, u32[]{:S(2)}) async-start(bf16[8,1,64,8,512]{4,3,0,1,2:T(8,128)(2,1)} %copy.8), calls=%async_computation.1 | async-start | bytes 8388608 | tf_op jit(solution)/shard_map/all_to_all | solution.py:79
  374.0 26.9 %collective-permute-start = (f32[512,512]{1,0:T(8,128)S(1)}, f32[512,512]{1,0:T(8,128)S(1)}, u32[]{:S(2)}, u32[]{:S(2)}) collective-permute-start(f32[512,512]{1,0:T(8,128)S(1)} %fusion.17), channel_id=1, source_target_pairs={{0,1},{1,0},{2,3},{3,2},{4,5},{5,4},{6,7},{7,6},{8,9},{9,8},{10,11... | collective-permute-start | bytes 3145736 | tf_op jit(solution)/shard_map/ppermute | solution.py:17
  401.1 49.4 %collective-permute-start.1 = (f32[512,512]{1,0:T(8,128)S(1)}, f32[512,512]{1,0:T(8,128)S(1)}, u32[]{:S(2)}, u32[]{:S(2)}) collective-permute-start(f32[512,512]{1,0:T(8,128)S(1)} %add.113), channel_id=1, source_target_pairs={{0,2},{1,3},{2,0},{3,1},{4,6},{5,7},{6,4},{7,5},{8,10},{9,11},{10,... | collective-permute-start | bytes 3145736 | tf_op jit(solution)/shard_map/ppermute | solution.py:17
  450.7 96.2 %collective-permute-start.2 = (f32[512,512]{1,0:T(8,128)S(1)}, f32[512,512]{1,0:T(8,128)S(1)}, u32[]{:S(2)}, u32[]{:S(2)}) collective-permute-start(f32[512,512]{1,0:T(8,128)S(1)} %add.114), channel_id=1, source_target_pairs={{0,4},{1,5},{2,6},{3,7},{4,0},{5,1},{6,2},{7,3},{8,12},{9,13},{10,... | collective-permute-start | bytes 3145736 | tf_op jit(solution)/shard_map/ppermute | solution.py:17
  548.4 27.0 %collective-permute-start.3 = (f32[512,512]{1,0:T(8,128)S(1)}, f32[512,512]{1,0:T(8,128)S(1)}, u32[]{:S(2)}, u32[]{:S(2)}) collective-permute-start(f32[512,512]{1,0:T(8,128)S(1)} %fusion.18), channel_id=1, source_target_pairs={{0,1},{1,0},{2,3},{3,2},{4,5},{5,4},{6,7},{7,6},{8,9},{9,8},{10,11... | collective-permute-start | bytes 3145736 | tf_op jit(solution)/shard_map/ppermute | solution.py:17
  575.6 49.5 %collective-permute-start.4 = (f32[512,512]{1,0:T(8,128)S(1)}, f32[512,512]{1,0:T(8,128)S(1)}, u32[]{:S(2)}, u32[]{:S(2)}) collective-permute-start(f32[512,512]{1,0:T(8,128)S(1)} %add.118), channel_id=1, source_target_pairs={{0,2},{1,3},{2,0},{3,1},{4,6},{5,7},{6,4},{7,5},{8,10},{9,11},{10,... | collective-permute-start | bytes 3145736 | tf_op jit(solution)/shard_map/ppermute | solution.py:17
  625.3 94.4 %collective-permute-start.5 = (f32[512,512]{1,0:T(8,128)S(1)}, f32[512,512]{1,0:T(8,128)S(1)}, u32[]{:S(2)}, u32[]{:S(2)}) collective-permute-start(f32[512,512]{1,0:T(8,128)S(1)} %add.119), channel_id=1, source_target_pairs={{0,4},{1,5},{2,6},{3,7},{4,0},{5,1},{6,2},{7,3},{8,12},{9,13},{10,... | collective-permute-start | bytes 3145736 | tf_op jit(solution)/shard_map/ppermute | solution.py:17
  721.3 27.0 %collective-permute-start.6 = (f32[512,512]{1,0:T(8,128)S(1)}, f32[512,512]{1,0:T(8,128)S(1)}, u32[]{:S(2)}, u32[]{:S(2)}) collective-permute-start(f32[512,512]{1,0:T(8,128)S(1)} %fusion.19), channel_id=1, source_target_pairs={{0,1},{1,0},{2,3},{3,2},{4,5},{5,4},{6,7},{7,6},{8,9},{9,8},{10,11... | collective-permute-start | bytes 3145736 | tf_op jit(solution)/shard_map/ppermute | solution.py:17
  748.4 49.5 %collective-permute-start.7 = (f32[512,512]{1,0:T(8,128)S(1)}, f32[512,512]{1,0:T(8,128)S(1)}, u32[]{:S(2)}, u32[]{:S(2)}) collective-permute-start(f32[512,512]{1,0:T(8,128)S(1)} %add.123), channel_id=1, source_target_pairs={{0,2},{1,3},{2,0},{3,1},{4,6},{5,7},{6,4},{7,5},{8,10},{9,11},{10,... | collective-permute-start | bytes 3145736 | tf_op jit(solution)/shard_map/ppermute | solution.py:17
  798.1 94.4 %collective-permute-start.8 = (f32[512,512]{1,0:T(8,128)S(1)}, f32[512,512]{1,0:T(8,128)S(1)}, u32[]{:S(2)}, u32[]{:S(2)}) collective-permute-start(f32[512,512]{1,0:T(8,128)S(1)} %add.124), channel_id=1, source_target_pairs={{0,4},{1,5},{2,6},{3,7},{4,0},{5,1},{6,2},{7,3},{8,12},{9,13},{10,... | collective-permute-start | bytes 3145736 | tf_op jit(solution)/shard_map/ppermute | solution.py:17
  894.3 41.7 %all-to-all-start.2 = ((bf16[1,64,8,512]{3,2,0,1:T(8,128)(2,1)}), bf16[1,64,8,512]{3,2,0,1:T(8,128)(2,1)S(1)}, u32[]{:S(2)}, u32[]{:S(2)}) async-start(bf16[1,64,8,512]{3,2,0,1:T(8,128)(2,1)} %bitcast.6), calls=%async_computation.2 | async-start | bytes 1048576 | tf_op jit(solution)/shard_map/all_to_all | solution.py:105
where the time goes:
time: 938 us; the launch traced here: 937 us
  waiting for transfers between devices  697 us (74%)
  blocking collectives  154 us (16%)
  starting transfers between devices  56 us (6%)
  other arithmetic  18.9 us (2%)
    ppermute x9, waiting for transfers between devices, partner(): lax.ppermute(shard, axis, [(i, i ^ 1 << stride) for i in range(lax.axis_s...  487 us
    all_to_all x1, waiting for transfers between devices, body(): lax.all_to_all(lax.all_to_all(sectioned, 'domain', split_axis=1, concat_a...  182 us
    psum x1, blocking collectives, share_scores(): return lax.psum((aligned, squares, norm_slots), ('domain', 'fsdp'))  99.8 us
    all_to_all x1, blocking collectives, body(): lax.all_to_all(sectioned, 'domain', split_axis=1, concat_axis=0, tiled=True)  54.6 us
    all_to_all x1, waiting for transfers between devices, body(): lax.all_to_all(finished.reshape(1, shards, sub_rows, columns), 'fsdp', sp...  27.8 us
    ppermute x9, starting transfers between devices, partner(): lax.ppermute(shard, axis, [(i, i ^ 1 << stride) for i in range(lax.axis_s...  27.1 us
    all_to_all x1, starting transfers between devices, body(): lax.all_to_all(lax.all_to_all(sectioned, 'domain', split_axis=1, concat_a...  19.1 us
  transfers between devices with their start and end apart: 11, of which 11 were waited for; matrix products, arithmetic and copies ran while one was open for 1% of the time, Pallas kernels for 0%

commit v1 on v0

--- a/solution.py
+++ b/solution.py
@@ -11,6 +11,11 @@
 COEF_C = 2.0315
 MUON_SCALE = 0.2
 ETA = 4.0
+
+
+def bring_the_set(target, axis_id, chip_axis):
+    s_next = lax.psum(lax.psum(target, axis_name=axis_id), axis_name=chip_axis)
+    return s_next
 
 
 def partner(shard, axis, stride):
@@ -52,7 +57,7 @@
 
 
 def share_scores(aligned, squares, norm_slots):
-    return lax.psum((aligned, squares, norm_slots), ("domain", "fsdp"))
+    return bring_the_set((aligned, squares, norm_slots), "domain", "fsdp")
 
 
 def body(gradients, row_counts, domain_ids, domain_weights):

time: 938 us -> 879 us (0.937)
  waiting for transfers between devices: 697 us -> 540 us
  starting transfers between devices: 56 us -> 120 us
  blocking collectives: 154 us -> 188 us
    ppermute x9, waiting for transfers between devices: 487 us -> 340 us  [partner(): lax.ppermute(shard, axis, [(i, i ^ 1 << stride) for i in range(lax.axis_s...]
    ppermute x9, starting transfers between devices: 27.1 us -> 74.3 us  [partner(): lax.ppermute(shard, axis, [(i, i ^ 1 << stride) for i in range(lax.axis_s...]
    psum x1 -> x2, blocking collectives: 99.8 us -> 134 us  [bring_the_set(): s_next = lax.psum(lax.psum(target, axis_name=axis_id), axis_name=chip_axis)]
    all_to_all x1, starting transfers between devices: 9.81 us -> 27 us  [body(): lax.all_to_all(finished.reshape(1, shards, sub_rows, columns), 'fsdp', sp...]
    all_to_all x1, waiting for transfers between devices: 27.8 us -> 17.6 us  [body(): lax.all_to_all(finished.reshape(1, shards, sub_rows, columns), 'fsdp', sp...]
where the time goes in v1:
time: 879 us; the launch traced here: 878 us
  waiting for transfers between devices  540 us (61%)
  blocking collectives  188 us (21%)
  starting transfers between devices  120 us (14%)
  other arithmetic  18.9 us (2%)
    ppermute x9, waiting for transfers between devices, partner(): lax.ppermute(shard, axis, [(i, i ^ 1 << stride) for i in range(lax.axis_s...  340 us
    all_to_all x1, waiting for transfers between devices, body(): lax.all_to_all(lax.all_to_all(sectioned, 'domain', split_axis=1, concat_a...  182 us
    psum x2, blocking collectives, bring_the_set(): s_next = lax.psum(lax.psum(target, axis_name=axis_id), axis_name=chip_axis)  134 us
    ppermute x9, starting transfers between devices, partner(): lax.ppermute(shard, axis, [(i, i ^ 1 << stride) for i in range(lax.axis_s...  74.3 us
    all_to_all x1, blocking collectives, body(): lax.all_to_all(sectioned, 'domain', split_axis=1, concat_axis=0, tiled=True)  54.6 us
    all_to_all x1, starting transfers between devices, body(): lax.all_to_all(finished.reshape(1, shards, sub_rows, columns), 'fsdp', sp...  27 us
    all_to_all x1, starting transfers between devices, body(): lax.all_to_all(lax.all_to_all(sectioned, 'domain', split_axis=1, concat_a...  19.1 us
    all_to_all x1, waiting for transfers between devices, body(): lax.all_to_all(finished.reshape(1, shards, sub_rows, columns), 'fsdp', sp...  17.6 us
  transfers between devices with their start and end apart: 11, of which 11 were waited for; matrix products, arithmetic and copies ran while one was open for 1% of the time, Pallas kernels for 0%

profile of v1, /device:TPU:8, one launch (start us, length us, event | category | flops | bytes accessed | tf_op | source)
XLA Modules:
  0.0 878.4 jit_solution(14256214146503913212)
XLA Ops:
  0.6 54.6 %all_to_all.30 = bf16[1,8,64,8,512]{4,3,2,0,1:T(8,128)(2,1)S(1)} all-to-all(bf16[1,8,64,8,512]{4,3,2,0,1:T(8,128)(2,1)} %bitcast.26), channel_id=1, replica_groups=mesh['domain'=8,'fsdp'=64] {'domain'}, dimensions={1} | all-to-all | bytes 8388608 | tf_op jit(solution)/shard_map/all_to_all | solution.py:85
  55.3 2.6 copy.8
  57.9 19.1 %all-to-all-start.1 = ((bf16[8,1,64,8,512]{4,3,0,1,2:T(8,128)(2,1)}), bf16[8,1,64,8,512]{4,3,0,1,2:T(8,128)(2,1)}, u32[]{:S(2)}, u32[]{:S(2)}) async-start(bf16[8,1,64,8,512]{4,3,0,1,2:T(8,128)(2,1)} %copy.8), calls=%async_computation.1 | async-start | bytes 8388608 | tf_op jit(solution)/shard_map/all_to_all | solution.py:84
  79.8 182.4 %all-to-all-done.1 = bf16[8,1,64,8,512]{4,3,0,1,2:T(8,128)(2,1)} async-done(((bf16[8,1,64,8,512]{4,3,0,1,2:T(8,128)(2,1)}), bf16[8,1,64,8,512]{4,3,0,1,2:T(8,128)(2,1)}, u32[]{:S(2)}, u32[]{:S(2)}) %all-to-all-start.1) | async-done | bytes 4194336 | tf_op jit(solution)/shard_map/all_to_all | solution.py:84
  262.2 4.3 multiply_reduce_fusion.2
  268.0 4.3 multiply_reduce_fusion
  272.3 12.4 %all-reduce.1 = (f32[64]{0:T(128)S(1)}, f32[8]{0:T(128)S(1)}, f32[8]{0:T(128)S(1)}) all-reduce(f32[64]{0:T(128)S(1)} %compare_select_fusion, f32[8]{0:T(128)S(1)} %get-tuple-element.3, f32[8]{0:T(128)S(1)} %get-tuple-element.2), channel_id=1, replica_groups=mesh['domain'=8,'fsdp'=64] {'domain'}, use_global_device_ids=true, to_apply=%region_5.6 | all-reduce | flops 80 | bytes 640 | tf_op jit(solution)/shard_map/psum | solution.py:17
  284.7 121.4 %all-reduce = (f32[64]{0:T(128)S(1)}, f32[8]{0:T(128)S(1)}, f32[8]{0:T(128)S(1)}) all-reduce(f32[64]{0:T(128)S(1)} %get-tuple-element.7, f32[8]{0:T(128)S(1)} %get-tuple-element.8, f32[8]{0:T(128)S(1)} %get-tuple-element.9), channel_id=1, replica_groups=mesh['domain'=8,'fsdp'=64] {'fsdp'}, use_global_device_ids=true, to_apply=%region_6.7 | all-reduce | flops 80 | bytes 640 | tf_op jit(solution)/shard_map/psum | solution.py:17
  409.9 25.2 %collective-permute-done = f32[512,512]{1,0:T(8,128)S(1)} collective-permute-done((f32[512,512]{1,0:T(8,128)S(1)}, f32[512,512]{1,0:T(8,128)S(1)}, u32[]{:S(2)}, u32[]{:S(2)}) %collective-permute-start) | collective-permute-done | bytes 1048608 | tf_op jit(solution)/shard_map/ppermute | solution.py:22
  435.3 31.1 %collective-permute-start.1 = (f32[512,512]{1,0:T(8,128)S(1)}, f32[512,512]{1,0:T(8,128)S(1)}, u32[]{:S(2)}, u32[]{:S(2)}) collective-permute-start(f32[512,512]{1,0:T(8,128)S(1)} %add.119), channel_id=1, source_target_pairs={{0,2},{1,3},{2,0},{3,1},{4,6},{5,7},{6,4},{7,5},{8,10},{9,11},{10,... | collective-permute-start | bytes 3145736 | tf_op jit(solution)/shard_map/ppermute | solution.py:22
  466.4 31.7 %collective-permute-done.1 = f32[512,512]{1,0:T(8,128)S(1)} collective-permute-done((f32[512,512]{1,0:T(8,128)S(1)}, f32[512,512]{1,0:T(8,128)S(1)}, u32[]{:S(2)}, u32[]{:S(2)}) %collective-permute-start.1) | collective-permute-done | bytes 1048608 | tf_op jit(solution)/shard_map/ppermute | solution.py:22
  498.3 1.9 collective-permute-start.2
  500.2 51.2 %collective-permute-done.2 = f32[512,512]{1,0:T(8,128)S(1)} collective-permute-done((f32[512,512]{1,0:T(8,128)S(1)}, f32[512,512]{1,0:T(8,128)S(1)}, u32[]{:S(2)}, u32[]{:S(2)}) %collective-permute-start.2) | collective-permute-done | bytes 1048608 | tf_op jit(solution)/shard_map/ppermute | solution.py:22
  554.9 21.2 %collective-permute-done.3 = f32[512,512]{1,0:T(8,128)S(1)} collective-permute-done((f32[512,512]{1,0:T(8,128)S(1)}, f32[512,512]{1,0:T(8,128)S(1)}, u32[]{:S(2)}, u32[]{:S(2)}) %collective-permute-start.3) | collective-permute-done | bytes 1048608 | tf_op jit(solution)/shard_map/ppermute | solution.py:22
  576.3 26.6 %collective-permute-start.4 = (f32[512,512]{1,0:T(8,128)S(1)}, f32[512,512]{1,0:T(8,128)S(1)}, u32[]{:S(2)}, u32[]{:S(2)}) collective-permute-start(f32[512,512]{1,0:T(8,128)S(1)} %add.124), channel_id=1, source_target_pairs={{0,2},{1,3},{2,0},{3,1},{4,6},{5,7},{6,4},{7,5},{8,10},{9,11},{10,... | collective-permute-start | bytes 3145736 | tf_op jit(solution)/shard_map/ppermute | solution.py:22
  602.9 23.8 %collective-permute-done.4 = f32[512,512]{1,0:T(8,128)S(1)} collective-permute-done((f32[512,512]{1,0:T(8,128)S(1)}, f32[512,512]{1,0:T(8,128)S(1)}, u32[]{:S(2)}, u32[]{:S(2)}) %collective-permute-start.4) | collective-permute-done | bytes 1048608 | tf_op jit(solution)/shard_map/ppermute | solution.py:22
  626.9 3.7 collective-permute-start.5
  630.6 84.6 %collective-permute-done.5 = f32[512,512]{1,0:T(8,128)S(1)} collective-permute-done((f32[512,512]{1,0:T(8,128)S(1)}, f32[512,512]{1,0:T(8,128)S(1)}, u32[]{:S(2)}, u32[]{:S(2)}) %collective-permute-start.5) | collective-permute-done | bytes 1048608 | tf_op jit(solution)/shard_map/ppermute | solution.py:22
  718.6 18.2 %collective-permute-done.6 = f32[512,512]{1,0:T(8,128)S(1)} collective-permute-done((f32[512,512]{1,0:T(8,128)S(1)}, f32[512,512]{1,0:T(8,128)S(1)}, u32[]{:S(2)}, u32[]{:S(2)}) %collective-permute-start.6) | collective-permute-done | bytes 1048608 | tf_op jit(solution)/shard_map/ppermute | solution.py:22
  739.0 37.0 %collective-permute-done.7 = f32[512,512]{1,0:T(8,128)S(1)} collective-permute-done((f32[512,512]{1,0:T(8,128)S(1)}, f32[512,512]{1,0:T(8,128)S(1)}, u32[]{:S(2)}, u32[]{:S(2)}) %collective-permute-start.7) | collective-permute-done | bytes 1048608 | tf_op jit(solution)/shard_map/ppermute | solution.py:22
  776.2 3.3 collective-permute-start.8
  779.5 47.3 %collective-permute-done.8 = f32[512,512]{1,0:T(8,128)S(1)} collective-permute-done((f32[512,512]{1,0:T(8,128)S(1)}, f32[512,512]{1,0:T(8,128)S(1)}, u32[]{:S(2)}, u32[]{:S(2)}) %collective-permute-start.8) | collective-permute-done | bytes 1048608 | tf_op jit(solution)/shard_map/ppermute | solution.py:22
  828.6 27.0 %all-to-all-start.2 = ((bf16[1,64,8,512]{3,2,0,1:T(8,128)(2,1)}), bf16[1,64,8,512]{3,2,0,1:T(8,128)(2,1)S(1)}, u32[]{:S(2)}, u32[]{:S(2)}) async-start(bf16[1,64,8,512]{3,2,0,1:T(8,128)(2,1)} %bitcast.6), calls=%async_computation.2 | async-start | bytes 1048576 | tf_op jit(solution)/shard_map/all_to_all | solution.py:110
  859.7 17.6 %all-to-all-done.2 = bf16[1,64,8,512]{3,2,0,1:T(8,128)(2,1)S(1)} async-done(((bf16[1,64,8,512]{3,2,0,1:T(8,128)(2,1)}), bf16[1,64,8,512]{3,2,0,1:T(8,128)(2,1)S(1)}, u32[]{:S(2)}, u32[]{:S(2)}) %all-to-all-start.2) | async-done | bytes 524320 | tf_op jit(solution)/shard_map/all_to_all | solution.py:110
  (42 shorter events, 23.7 us)
Async XLA Ops:
  57.9 19.1 %copy-start = (f32[8]{0:T(128)S(1)}, f32[8]{0:T(128)}, u32[]{:S(2)}) copy-start(f32[8]{0:T(128)} %param.7) | copy-start | bytes 100
  57.9 19.7 %copy-start.1 = (s32[64]{0:T(128)S(1)}, s32[64]{0:T(128)}, u32[]{:S(2)}) copy-start(s32[64]{0:T(128)} %param.5) | copy-start | bytes 772
  57.9 20.3 %copy-start.2 = (s32[8]{0:T(128)S(1)}, s32[8]{0:T(128)}, u32[]{:S(2)}) copy-start(s32[8]{0:T(128)} %param.6) | copy-start | bytes 100
  57.9 204.3 %all-to-all-start.1 = ((bf16[8,1,64,8,512]{4,3,0,1,2:T(8,128)(2,1)}), bf16[8,1,64,8,512]{4,3,0,1,2:T(8,128)(2,1)}, u32[]{:S(2)}, u32[]{:S(2)}) async-start(bf16[8,1,64,8,512]{4,3,0,1,2:T(8,128)(2,1)} %copy.8), calls=%async_computation.1 | async-start | bytes 8388608 | tf_op jit(solution)/shard_map/all_to_all | solution.py:84
  408.0 27.1 %collective-permute-start = (f32[512,512]{1,0:T(8,128)S(1)}, f32[512,512]{1,0:T(8,128)S(1)}, u32[]{:S(2)}, u32[]{:S(2)}) collective-permute-start(f32[512,512]{1,0:T(8,128)S(1)} %fusion.17), channel_id=1, source_target_pairs={{0,1},{1,0},{2,3},{3,2},{4,5},{5,4},{6,7},{7,6},{8,9},{9,8},{10,11... | collective-permute-start | bytes 3145736 | tf_op jit(solution)/shard_map/ppermute | solution.py:22
  435.3 62.8 %collective-permute-start.1 = (f32[512,512]{1,0:T(8,128)S(1)}, f32[512,512]{1,0:T(8,128)S(1)}, u32[]{:S(2)}, u32[]{:S(2)}) collective-permute-start(f32[512,512]{1,0:T(8,128)S(1)} %add.119), channel_id=1, source_target_pairs={{0,2},{1,3},{2,0},{3,1},{4,6},{5,7},{6,4},{7,5},{8,10},{9,11},{10,... | collective-permute-start | bytes 3145736 | tf_op jit(solution)/shard_map/ppermute | solution.py:22
  498.3 53.2 %collective-permute-start.2 = (f32[512,512]{1,0:T(8,128)S(1)}, f32[512,512]{1,0:T(8,128)S(1)}, u32[]{:S(2)}, u32[]{:S(2)}) collective-permute-start(f32[512,512]{1,0:T(8,128)S(1)} %add.120), channel_id=1, source_target_pairs={{0,4},{1,5},{2,6},{3,7},{4,0},{5,1},{6,2},{7,3},{8,12},{9,13},{10,... | collective-permute-start | bytes 3145736 | tf_op jit(solution)/shard_map/ppermute | solution.py:22
  553.0 23.1 %collective-permute-start.3 = (f32[512,512]{1,0:T(8,128)S(1)}, f32[512,512]{1,0:T(8,128)S(1)}, u32[]{:S(2)}, u32[]{:S(2)}) collective-permute-start(f32[512,512]{1,0:T(8,128)S(1)} %fusion.18), channel_id=1, source_target_pairs={{0,1},{1,0},{2,3},{3,2},{4,5},{5,4},{6,7},{7,6},{8,9},{9,8},{10,11... | collective-permute-start | bytes 3145736 | tf_op jit(solution)/shard_map/ppermute | solution.py:22
  576.3 50.4 %collective-permute-start.4 = (f32[512,512]{1,0:T(8,128)S(1)}, f32[512,512]{1,0:T(8,128)S(1)}, u32[]{:S(2)}, u32[]{:S(2)}) collective-permute-start(f32[512,512]{1,0:T(8,128)S(1)} %add.124), channel_id=1, source_target_pairs={{0,2},{1,3},{2,0},{3,1},{4,6},{5,7},{6,4},{7,5},{8,10},{9,11},{10,... | collective-permute-start | bytes 3145736 | tf_op jit(solution)/shard_map/ppermute | solution.py:22
  626.9 88.3 %collective-permute-start.5 = (f32[512,512]{1,0:T(8,128)S(1)}, f32[512,512]{1,0:T(8,128)S(1)}, u32[]{:S(2)}, u32[]{:S(2)}) collective-permute-start(f32[512,512]{1,0:T(8,128)S(1)} %add.125), channel_id=1, source_target_pairs={{0,4},{1,5},{2,6},{3,7},{4,0},{5,1},{6,2},{7,3},{8,12},{9,13},{10,... | collective-permute-start | bytes 3145736 | tf_op jit(solution)/shard_map/ppermute | solution.py:22
  716.7 20.1 %collective-permute-start.6 = (f32[512,512]{1,0:T(8,128)S(1)}, f32[512,512]{1,0:T(8,128)S(1)}, u32[]{:S(2)}, u32[]{:S(2)}) collective-permute-start(f32[512,512]{1,0:T(8,128)S(1)} %fusion.19), channel_id=1, source_target_pairs={{0,1},{1,0},{2,3},{3,2},{4,5},{5,4},{6,7},{7,6},{8,9},{9,8},{10,11... | collective-permute-start | bytes 3145736 | tf_op jit(solution)/shard_map/ppermute | solution.py:22
  737.1 39.0 %collective-permute-start.7 = (f32[512,512]{1,0:T(8,128)S(1)}, f32[512,512]{1,0:T(8,128)S(1)}, u32[]{:S(2)}, u32[]{:S(2)}) collective-permute-start(f32[512,512]{1,0:T(8,128)S(1)} %add.129), channel_id=1, source_target_pairs={{0,2},{1,3},{2,0},{3,1},{4,6},{5,7},{6,4},{7,5},{8,10},{9,11},{10,... | collective-permute-start | bytes 3145736 | tf_op jit(solution)/shard_map/ppermute | solution.py:22
  776.2 50.6 %collective-permute-start.8 = (f32[512,512]{1,0:T(8,128)S(1)}, f32[512,512]{1,0:T(8,128)S(1)}, u32[]{:S(2)}, u32[]{:S(2)}) collective-permute-start(f32[512,512]{1,0:T(8,128)S(1)} %add.130), channel_id=1, source_target_pairs={{0,4},{1,5},{2,6},{3,7},{4,0},{5,1},{6,2},{7,3},{8,12},{9,13},{10,... | collective-permute-start | bytes 3145736 | tf_op jit(solution)/shard_map/ppermute | solution.py:22
  828.6 48.7 %all-to-all-start.2 = ((bf16[1,64,8,512]{3,2,0,1:T(8,128)(2,1)}), bf16[1,64,8,512]{3,2,0,1:T(8,128)(2,1)S(1)}, u32[]{:S(2)}, u32[]{:S(2)}) async-start(bf16[1,64,8,512]{3,2,0,1:T(8,128)(2,1)} %bitcast.6), calls=%async_computation.2 | async-start | bytes 1048576 | tf_op jit(solution)/shard_map/all_to_all | solution.py:110
